TPU v7x, 1024 devices: a whole 4x8x16 slice. The times are simulated.
1024 devices in a mesh: tok: 16 (over x_lo, y), dmod: 4 (over x_hi, core), hid: 16 (over z).
Axes of the slice: x: 4 (x_hi: 2, x_lo: 2; x = x_hi * 2 + x_lo), y: 8, z: 16, core: 2. Of those that a mesh axis runs over, the one named last changes fastest.
Arguments:
- inputs: bfloat16 [1536, 8192], P('dmod', 'tok'), may hold values from -6 to 6
- grad_hidden: bfloat16 [1536, 14336], P('dmod', 'hid'), may hold values from -6 to 6
- gate_weight: bfloat16 [8192, 14336], P(('tok', 'dmod'), 'hid'), may hold values from -0.0625 to 0.0625
- up_weight: bfloat16 [8192, 14336], P(('tok', 'dmod'), 'hid'), may hold values from -0.0625 to 0.0625
Outputs:
- grad_inputs: bfloat16 [1536, 8192], P(('dmod', 'hid'), 'tok')
- grad_gate_weight: bfloat16 [8192, 14336], P(('tok', 'dmod'), 'hid')
- grad_up_weight: bfloat16 [8192, 14336], P(('tok', 'dmod'), 'hid')
All inputs are finite; a program needn't handle non-finite values.
Results may differ from a plain program's by a relative error of at most 0.0049.
Values may be sent and summed in bfloat16 or wider, within the bound.
A program may use at most 32 MiB of HBM per device.

v0:
```python
import jax
import jax.numpy as jnp
from jax import lax
from jax.sharding import PartitionSpec as P


def derive(gate, up, upstream):
    sigma = jax.nn.sigmoid(gate)
    upstream = upstream.astype(jnp.float32)
    grad_gate = (upstream * up * sigma * (1.0 + gate * (1.0 - sigma))).astype(jnp.bfloat16)
    grad_up = (upstream * gate * sigma).astype(jnp.bfloat16)
    return (grad_gate, grad_up)


def shards(inputs, grad_hidden, gate_weight, up_weight):
    gate_block, up_block = (
        lax.all_gather(gate_weight, "dmod", axis=0, tiled=True),
        lax.all_gather(up_weight, "dmod", axis=0, tiled=True),
    )
    gate_part = jnp.dot(inputs, gate_block, preferred_element_type=jnp.float32)
    up_part = jnp.dot(inputs, up_block, preferred_element_type=jnp.float32)
    position = lax.axis_index("tok")
    gate_share, up_share = (
        lax.psum_scatter(gate_part, "tok", scatter_dimension=1, tiled=True),
        lax.psum_scatter(up_part, "tok", scatter_dimension=1, tiled=True),
    )
    width = gate_share.shape[1]
    upstream = lax.dynamic_slice_in_dim(grad_hidden, position * width, width, 1)
    grad_gate, grad_up = derive(gate_share, up_share, upstream)
    grad_gate, grad_up = (
        lax.all_gather(grad_gate, "tok", axis=1, tiled=True),
        lax.all_gather(grad_up, "tok", axis=1, tiled=True),
    )
    partial_inputs = jnp.einsum(
        "tf,df->td", grad_gate, gate_block, preferred_element_type=jnp.float32
    )
    partial_inputs = partial_inputs + jnp.einsum(
        "tf,df->td", grad_up, up_block, preferred_element_type=jnp.float32
    )
    grad_inputs = lax.psum_scatter(partial_inputs, "hid", scatter_dimension=0, tiled=True).astype(
        jnp.bfloat16
    )
    partial_gate_w = jnp.einsum("td,tf->df", inputs, grad_gate, preferred_element_type=jnp.float32)
    partial_up_w = jnp.einsum("td,tf->df", inputs, grad_up, preferred_element_type=jnp.float32)
    summed_gate_w, summed_up_w = (
        lax.psum_scatter(partial_gate_w, "dmod", scatter_dimension=0, tiled=True),
        lax.psum_scatter(partial_up_w, "dmod", scatter_dimension=0, tiled=True),
    )
    return (grad_inputs, summed_gate_w.astype(jnp.bfloat16), summed_up_w.astype(jnp.bfloat16))


def solution(mesh):
    placed = (
        P("dmod", "tok"),
        P("dmod", "hid"),
        P(("tok", "dmod"), "hid"),
        P(("tok", "dmod"), "hid"),
    )
    return jax.shard_map(
        shards,
        mesh=mesh,
        in_specs=placed,
        out_specs=(P(("dmod", "hid"), "tok"), P(("tok", "dmod"), "hid"), P(("tok", "dmod"), "hid")),
        check_vma=False,
    )
```

profile of v0, /device:TPU:1, one launch (start us, length us, event | category | flops | bytes accessed | tf_op | source)
XLA Modules:
  0.0 462.5 jit_solution(17961600557134718370)
XLA Ops:
  7.2 0.0 reduce-scatter.18.cloned.1.call-start
  7.2 23.4 %all_gather.12 = bf16[512,896]{1,0:T(8,128)(2,1)S(1)} all-gather(bf16[128,896]{1,0:T(8,128)(2,1)} %param.7), channel_id=1, replica_groups=mesh['tok'=16,'dmod'=4,'hid'=16] {'dmod'}, dimensions={0}, use_global_device_ids=true | all-gather | bytes 1146880 | tf_op jit(solution)/shard_map/all_gather | solution.py:18
  30.7 2.8 fusion.5
  33.5 0.0 reduce-scatter.18.cloned.1.call-update
  33.5 0.0 reduce-scatter.20.cloned.1.call-start
  33.6 11.1 %all_gather.13 = bf16[512,896]{1,0:T(8,128)(2,1)S(1)} all-gather(bf16[128,896]{1,0:T(8,128)(2,1)S(1)} %copy-done.4), channel_id=1, replica_groups=mesh['tok'=16,'dmod'=4,'hid'=16] {'dmod'}, dimensions={0}, use_global_device_ids=true | all-gather | bytes 1146880 | tf_op jit(solution)/shard_map/all_gather | solution.py:17
  44.7 1.8 fusion.6
  46.4 0.0 reduce-scatter.20.cloned.1.call-update
  46.5 0.0 reduce-scatter.12.cloned.1.call-start
  46.5 0.1 constant_dynamic-slice_fusion
  46.6 0.1 copy.13
  46.7 52.3 %reduce-scatter.18.cloned.1.call-done = f32[384,56]{0,1:T(8,128)} async-done(((f32[384,896]{0,1:T(8,128)}), f32[384,56]{0,1:T(8,128)}) %reduce-scatter.18.cloned.1.call-update) | async-done | bytes 86032
  99.1 80.2 %reduce-scatter.20.cloned.1.call-done = f32[384,56]{0,1:T(8,128)} async-done(((f32[384,896]{0,1:T(8,128)}), f32[384,56]{0,1:T(8,128)}) %reduce-scatter.20.cloned.1.call-update) | async-done | bytes 86032
  179.3 1.0 fusion.4
  180.3 29.1 %all_gather.14 = bf16[384,896]{0,1:T(8,128)(2,1)S(1)} all-gather(bf16[384,56]{0,1:T(8,128)(2,1)S(1)} %get-tuple-element.10), channel_id=1, replica_groups=mesh['tok'=16,'dmod'=4,'hid'=16] {'tok'}, dimensions={1}, use_global_device_ids=true | all-gather | bytes 731136 | tf_op jit(solution)/shard_map/all_gather | solution.py:31
  209.3 0.6 fusion.7
  210.0 0.2 copy-done.2
  210.2 27.4 %all_gather.15 = bf16[384,896]{0,1:T(8,128)(2,1)S(1)} all-gather(bf16[384,56]{0,1:T(8,128)(2,1)S(1)} %get-tuple-element.9), channel_id=1, replica_groups=mesh['tok'=16,'dmod'=4,'hid'=16] {'tok'}, dimensions={1}, use_global_device_ids=true | all-gather | bytes 731136 | tf_op jit(solution)/shard_map/all_gather | solution.py:32
  237.6 1.5 convolution_add_fusion
  239.1 0.0 reduce-scatter.14.cloned.1.call-start
  239.2 1.9 convolution_bitcast_fusion.1
  241.1 0.0 reduce-scatter.14.cloned.1.call-update
  241.1 0.0 reduce-scatter.16.cloned.1.call-start
  241.1 1.9 convolution_bitcast_fusion
  243.0 79.8 %reduce-scatter.12.cloned.1.call-done = f32[24,512]{1,0:T(8,128)} async-done(((f32[384,512]{1,0:T(8,128)}), f32[24,512]{1,0:T(8,128)}) %reduce-scatter.12.cloned.1.call-update) | async-done | bytes 49168 | tf_op jit(solution)/shard_map/reduce_scatter | solution.py:40
  322.8 1.4 convert_element_type.21
  324.2 68.3 %reduce-scatter.14.cloned.1.call-done = f32[128,896]{0,1:T(8,128)} async-done(((f32[512,896]{0,1:T(8,128)}), f32[128,896]{0,1:T(8,128)}) %reduce-scatter.14.cloned.1.call-update) | async-done | bytes 458768 | tf_op jit(solution)/shard_map/reduce_scatter | solution.py:46
  392.5 1.0 convert_element_type.22
  393.6 0.8 copy.11
  394.4 59.7 %reduce-scatter.16.cloned.1.call-done = f32[128,896]{0,1:T(8,128)} async-done(((f32[512,896]{0,1:T(8,128)}), f32[128,896]{0,1:T(8,128)}) %reduce-scatter.16.cloned.1.call-update) | async-done | bytes 458768 | tf_op jit(solution)/shard_map/reduce_scatter | solution.py:47
  454.1 1.0 convert_element_type.23
  455.1 0.8 copy.12
  (11 shorter events, 0.1 us)
Async XLA Ops:
  7.2 39.4 %copy-start = (bf16[384,896]{1,0:T(8,128)(2,1)S(1)}, bf16[384,896]{1,0:T(8,128)(2,1)}, u32[]{:S(2)}) copy-start(bf16[384,896]{1,0:T(8,128)(2,1)} %param.5) | copy-start | bytes 2064388
  7.2 91.9 %reduce-scatter.18.cloned.1.call-start = ((), (), s32[]{:S(2)}) async-start(), calls=%async_computation.8 | async-start | bytes 1462272
  30.7 2.9 copy-start.4
  33.5 11.2 %copy-start.1 = (bf16[384,512]{1,0:T(8,128)(2,1)S(1)}, bf16[384,512]{1,0:T(8,128)(2,1)}, u32[]{:S(2)}) copy-start(bf16[384,512]{1,0:T(8,128)(2,1)} %param.4) | copy-start | bytes 1179652
  33.5 145.7 %reduce-scatter.20.cloned.1.call-start = ((), (), s32[]{:S(2)}) async-start(), calls=%async_computation.9 | async-start | bytes 1462272
  46.5 276.4 %reduce-scatter.12.cloned.1.call-start = ((), (), s32[]{:S(2)}) async-start(), calls=%async_computation.5 | async-start | bytes 835584 | tf_op jit(solution)/shard_map/reduce_scatter | solution.py:40
  209.3 0.9 copy-start.2
  237.6 1.6 copy-start.3
  239.1 153.4 %reduce-scatter.14.cloned.1.call-start = ((), (), s32[]{:S(2)}) async-start(), calls=%async_computation.6 | async-start | bytes 2293760 | tf_op jit(solution)/shard_map/reduce_scatter | solution.py:46
  241.1 213.0 %reduce-scatter.16.cloned.1.call-start = ((), (), s32[]{:S(2)}) async-start(), calls=%async_computation.7 | async-start | bytes 2293760 | tf_op jit(solution)/shard_map/reduce_scatter | solution.py:47
Sparse Core Ops, SparseCore 0:
  33.7 65.3 reduce-scatter.17
  102.5 76.7 reduce-scatter.19
  239.2 83.5 reduce-scatter.11
  326.8 65.7 reduce-scatter.13
  396.1 57.9 reduce-scatter.15
where the time goes:
time: 463 us; the launch traced here: 462 us
  waiting for transfers between devices  340 us (73%)
  blocking collectives  91 us (20%)
  between operations  13.8 us (3%)
  matrix products  10.5 us (2%)
    unnamed x7, waiting for transfers between devices  133 us
    reduce_scatter x1, waiting for transfers between devices, shards(): lax.psum_scatter(partial_inputs, 'hid', scatter_dimension=0, tiled=True)  79.8 us
    reduce_scatter x1, waiting for transfers between devices, shards(): lax.psum_scatter(partial_gate_w, 'dmod', scatter_dimension=0, tiled=True)  68.3 us
    reduce_scatter x1, waiting for transfers between devices, shards(): lax.psum_scatter(partial_up_w, 'dmod', scatter_dimension=0, tiled=True)  59.7 us
    all_gather x1, blocking collectives, shards(): lax.all_gather(grad_gate, 'tok', axis=1, tiled=True)  29.1 us
    all_gather x1, blocking collectives, shards(): lax.all_gather(grad_up, 'tok', axis=1, tiled=True)  27.4 us
    all_gather x1, blocking collectives, shards(): lax.all_gather(up_weight, 'dmod', axis=0, tiled=True)  23.4 us
    all_gather x1, blocking collectives, shards(): lax.all_gather(gate_weight, 'dmod', axis=0, tiled=True)  11.1 us
  transfers between devices with their start and end apart: 5, of which 5 were waited for; matrix products, arithmetic and copies ran while one was open for 2% of the time, Pallas kernels for 0%

commit v1 on v0

v1 whole, which is shorter than its diff:
```python
import functools

import jax
import jax.numpy as jnp
from jax import lax
from jax.experimental import pallas as pl
from jax.experimental.pallas import tpu as pltpu
from jax.sharding import PartitionSpec as P

BF, F32 = jnp.bfloat16, jnp.float32
LANES = 128


def contract(a, b, dims):
    return lax.dot_general(a, b, (dims, ((), ())), preferred_element_type=F32)


def widths(columns):
    tiles = columns // LANES
    return [2 * LANES] * (tiles // 2) + [LANES] * (tiles % 2)


def kernel(ny, nz, cols, x_ref, gh_ref, wg_ref, wu_ref, dx_ref, dwg_ref, dwu_ref, *scratch):
    n = len(cols)
    starts = [sum(cols[:i]) for i in range(n)]
    it = iter(scratch)
    take = lambda count: [next(it) for _ in range(count)]
    xs, xg, xt, ghs, zf, zs, zr, ze, fx = take(9)
    wb, pb, pr, yo, ys, yr, gb, dwf, dws, dwr = (take(n) for _ in range(10))
    x_s, x_r, gh_s, gh_r, z_s, z_r, f_s, f_r = take(8)
    w_s, w_r, p_s, p_r, y_s, y_r, g_s, g_r, k_s, k_r, d_s, d_r = take(12)

    tok, dmod, z = lax.axis_index("tok"), lax.axis_index("dmod"), lax.axis_index("hid")
    xl, y, xh, c = tok // ny, tok % ny, dmod // 2, dmod % 2
    other = 1 - c
    q = 2 * xl + xh
    tokens = x_ref.shape[0]
    share = tokens // (2 * ny)
    rows = tokens // nz
    home = c == xl

    def at(xl_=xl, xh_=xh, y_=y, c_=c, z_=z):
        return {"tok": xl_ * ny + y_, "dmod": xh_ * 2 + c_, "hid": z_}

    def send(src, dst, send_sem, recv_sem, target):
        copy = pltpu.make_async_remote_copy(
            src_ref=src, dst_ref=dst, send_sem=send_sem, recv_sem=recv_sem,
            device_id=target, device_id_type=pl.DeviceIdType.MESH,
        )
        copy.start()
        return copy

    def arrived(dst, sem):
        pltpu.make_async_copy(dst, dst, sem).wait()

    def block_of(k):
        qk = (q + k) % 4
        return qk, dict(xl_=qk // 2, xh_=qk % 2)

    pending = []

    barrier = pltpu.get_barrier_semaphore()
    peers = [at(c_=other), at(xl_=1 - xl, c_=other)]
    peers += [at(**block_of(k)[1]) for k in (1, 2, 3)]
    peers += [at(y_=(y + k) % ny) for k in range(1, ny)]
    peers += [at(z_=(z + k) % nz) for k in range(1, nz)]
    for peer in peers:
        pl.semaphore_signal(barrier, 1, device_id=peer, device_id_type=pl.DeviceIdType.MESH)

    for h in range(2):
        for cc in range(2):
            at_col = (2 * h + cc) * LANES
            xs[cc, h] = x_ref[:, at_col : at_col + LANES]
    for i in range(n):
        span = slice(starts[i], starts[i] + cols[i])
        wb[i][0, q] = wg_ref[:, span]
        wb[i][1, q] = wu_ref[:, span]

    @pl.when(home)
    def _():
        xg[xl] = xs[c]
        ghs[...] = gh_ref[c]

    pl.semaphore_wait(barrier, len(peers))

    to_core = (xs.at[other], xg.at[xl], x_s.at[0], x_r.at[0], at(c_=other))
    to_gh = (gh_ref.at[other], ghs, gh_s, gh_r, at(c_=other))
    to_chip = [
        (xs.at[cc], xg.at[xl], x_s.at[cc], x_r.at[1], at(xl_=1 - xl, c_=cc)) for cc in range(2)
    ]

    @pl.when(home)
    def _():
        send(*to_core)
        send(*to_gh)

    @pl.when(jnp.logical_not(home))
    def _():
        for args in to_chip:
            send(*args)

    for i in range(n):
        for k in (1, 3, 2):
            target = at(**block_of(k)[1])
            pending.append(
                send(wb[i].at[:, q], wb[i].at[:, q], w_s.at[i, k - 1], w_r.at[i, k - 1], target)
            )

    arrived(xg.at[1 - xl], x_r.at[1])

    @pl.when(jnp.logical_not(home))
    def _():
        arrived(xg.at[xl], x_r.at[0])
        arrived(ghs, gh_r)

    for b in range(4):
        xt[b] = xg[b // 2, b % 2].astype(F32).T.astype(BF)

    def partial(i):
        for k in (1, 2, 3):
            qk = (q + 4 - k) % 4
            arrived(wb[i].at[:, qk], w_r.at[i, k - 1])
        wide = jnp.concatenate([xg[b // 2, b % 2] for b in range(4)], axis=1)
        for m in range(2):
            w = wb[i][m].reshape(4 * LANES, cols[i])
            part = contract(wide, w, ((1,), (0,))).reshape(2, ny, share, cols[i])
            pb[i][:, :, m * share : (m + 1) * share] = part
        pending.append(send(pb[i].at[other], pr[i], p_s.at[i], p_r.at[i], at(c_=other)))

    def scatter(i):
        arrived(pr[i], p_r.at[i])
        ys[i][...] = (pb[i][c] + pr[i][...]).astype(BF)
        yo[i][...] = pb[i][c, y] + pr[i][y]
        for k in far_first:
            yk = (y + k) % ny
            pending.append(
                send(ys[i].at[yk], yr[i].at[k - 1], y_s.at[i, k - 1], y_r.at[i, k - 1], at(y_=yk))
            )

    far_first = sorted(range(1, ny), key=lambda k: -min(k, ny - k))

    def activate(i):
        total = yo[i][...]
        for k in far_first[::-1]:
            arrived(yr[i].at[k - 1], y_r.at[i, k - 1])
            total = total + yr[i][k - 1].astype(F32)
        gate, up = total[:share], total[share:]
        up_grad = ghs[:, starts[i] : starts[i] + cols[i]]
        sigma = jax.nn.sigmoid(gate)
        grad_gate = up_grad * up * sigma * (1.0 + gate * (1.0 - sigma))
        grad_up = up_grad * gate * sigma
        gb[i][c, y] = jnp.concatenate([grad_gate, grad_up], axis=0).astype(BF)
        for k in far_first:
            yk = (y + k) % ny
            block = gb[i].at[c, y]
            pending.append(send(block, block, g_s.at[i, k - 1], g_r.at[i, k - 1], at(y_=yk)))

    def gather(i):
        for k in far_first[::-1]:
            arrived(gb[i].at[c, (y + ny - k) % ny], g_r.at[i, k - 1])
        pending.append(send(gb[i].at[c], gb[i].at[c], k_s.at[i], k_r.at[i], at(c_=other)))

    def grads_of(i):
        both = gb[i][...].astype(F32).reshape(2 * ny, 2 * share, cols[i])
        grad_gate = both[:, :share].reshape(tokens, cols[i]).astype(BF)
        grad_up = both[:, share:].reshape(tokens, cols[i]).astype(BF)
        return grad_gate, grad_up

    def input_part(i):
        arrived(gb[i].at[other], k_r.at[i])
        for b in range(4):
            total = 0.0
            for m, grad in enumerate(grads_of(i)):
                total = total + contract(grad, wb[i][m, b], ((1,), (1,)))
            total = total.reshape(nz, rows, LANES)
            span = slice(b * rows, (b + 1) * rows)
            zf[:, span] = total if i == 0 else zf[:, span] + total

    def weight_part(i):
        for m, grad in enumerate(grads_of(i)):
            for b in range(4):
                dwf[i][b, m] = contract(xt[b], grad, ((1,), (0,)))
        dws[i][...] = dwf[i][...].astype(BF)
        for k in (2, 1, 3):
            qk, where = block_of(k)
            pending.append(
                send(dws[i].at[qk], dwr[i].at[k - 1], d_s.at[i, k - 1], d_r.at[i, k - 1], at(**where))
            )

    def weight_out(i):
        total = dwf[i][q]
        for k in (1, 3, 2):
            arrived(dwr[i].at[k - 1], d_r.at[i, k - 1])
            total = total + dwr[i][k - 1].astype(F32)
        span = slice(starts[i], starts[i] + cols[i])
        dwg_ref[:, span] = total[0].astype(BF)
        dwu_ref[:, span] = total[1].astype(BF)

    stages = [partial, scatter, activate, gather, input_part, weight_part]
    order = []
    for i in range(n):
        for at_step, stage in zip((0, 0.1, 1.2, 2.3, 2.4, 2.5), stages):
            order.append((i + at_step, i, stage))
    for _, i, stage in sorted(order, key=lambda entry: entry[0]):
        if i == n - 1 and stage is weight_part:
            z_far = sorted(range(1, nz), key=lambda k: -min(k, nz - k))
            zs[...] = zf[...].astype(BF)
            for k in z_far:
                zk = (z + k) % nz
                pending.append(
                    send(zs.at[zk], zr.at[k - 1], z_s.at[k - 1], z_r.at[k - 1], at(z_=zk))
                )
        stage(i)
    for i in range(n):
        weight_out(i)

    total = zf[z]
    for k in z_far[::-1]:
        arrived(zr.at[k - 1], z_r.at[k - 1])
        total = total + zr[k - 1].astype(F32)
    half = 2 * rows
    ze[...] = total.astype(BF).reshape(2, half, LANES)
    mine, theirs = ze.at[xl], ze.at[1 - xl]
    last = send(theirs, fx.at[c], f_s.at[0], f_r.at[c], at(xl_=1 - xl, c_=xl))
    on_chip = (mine, fx.at[c], f_s.at[1], f_r.at[c], at(c_=other))

    @pl.when(home)
    def _():
        fx[c] = ze[xl]

    @pl.when(jnp.logical_not(home))
    def _():
        send(*on_chip)
        arrived(fx.at[c], f_r.at[c])

    arrived(fx.at[other], f_r.at[other])
    for cc in range(2):
        got = fx[cc].astype(F32)
        for h in range(2):
            at_col = (2 * h + cc) * LANES
            dx_ref[:, at_col : at_col + LANES] = got[h * rows : (h + 1) * rows].astype(BF)

    def sent(src, sem):
        pltpu.make_async_copy(src, src, sem).wait()

    @pl.when(home)
    def _():
        sent(xs.at[other], x_s.at[0])
        sent(gh_ref.at[other], gh_s)

    @pl.when(jnp.logical_not(home))
    def _():
        for cc in range(2):
            sent(xs.at[cc], x_s.at[cc])
        sent(mine, f_s.at[1])

    last.wait_send()
    for copy in pending:
        copy.wait_send()


def shards(ny, nz, inputs, grad_hidden, gate_weight, up_weight):
    tokens, features = inputs.shape
    columns = gate_weight.shape[1]
    cols = widths(columns)
    n = len(cols)
    share, rows = tokens // (2 * ny), tokens // nz
    y = lax.axis_index("tok") % ny
    upstream = grad_hidden.reshape(2, ny, share, columns)
    upstream = lax.dynamic_index_in_dim(upstream, y, 1, keepdims=False).astype(F32)

    vmem = lambda shape, dtype: pltpu.VMEM(shape, dtype)
    scratch = [
        vmem((2, 2, tokens, LANES), BF),
        vmem((2, 2, tokens, LANES), BF),
        vmem((4, LANES, tokens), BF),
        vmem((share, columns), F32),
        vmem((nz, 4 * rows, LANES), F32),
        vmem((nz, 4 * rows, LANES), BF),
        vmem((nz - 1, 4 * rows, LANES), BF),
        vmem((2, 2 * rows, LANES), BF),
        vmem((2, 2 * rows, LANES), BF),
    ]
    for shape, dtype in (
        (lambda w: (2, 4, LANES, w), BF),
        (lambda w: (2, ny, 2 * share, w), F32),
        (lambda w: (ny, 2 * share, w), F32),
        (lambda w: (2 * share, w), F32),
        (lambda w: (ny, 2 * share, w), BF),
        (lambda w: (ny - 1, 2 * share, w), BF),
        (lambda w: (2, ny, 2 * share, w), BF),
        (lambda w: (4, 2, LANES, w), F32),
        (lambda w: (4, 2, LANES, w), BF),
        (lambda w: (3, 2, LANES, w), BF),
    ):
        scratch += [vmem(shape(w), dtype) for w in cols]
    dma = pltpu.SemaphoreType.DMA
    scratch += [dma((2,)), dma((2,)), dma, dma, dma((nz - 1,)), dma((nz - 1,)), dma((2,)), dma((2,))]
    for shape in ((n, 3), (n,), (n, ny - 1), (n, ny - 1), (n,), (n, 3)):
        scratch += [dma(shape), dma(shape)]

    in_vmem = pl.BlockSpec(memory_space=pltpu.VMEM)
    return pl.pallas_call(
        functools.partial(kernel, ny, nz, cols),
        out_shape=(
            jax.ShapeDtypeStruct((rows, features), BF),
            jax.ShapeDtypeStruct(gate_weight.shape, BF),
            jax.ShapeDtypeStruct(up_weight.shape, BF),
        ),
        in_specs=[in_vmem] * 4,
        out_specs=(in_vmem,) * 3,
        scratch_shapes=scratch,
        compiler_params=pltpu.CompilerParams(
            collective_id=0, has_side_effects=True, vmem_limit_bytes=40 * 2**20
        ),
        name="step",
    )(inputs, upstream, gate_weight, up_weight)


def solution(mesh):
    placed = (
        P("dmod", "tok"),
        P("dmod", "hid"),
        P(("tok", "dmod"), "hid"),
        P(("tok", "dmod"), "hid"),
    )
    return jax.shard_map(
        functools.partial(shards, mesh.shape["tok"] // 2, mesh.shape["hid"]),
        mesh=mesh,
        in_specs=placed,
        out_specs=(P(("dmod", "hid"), "tok"), P(("tok", "dmod"), "hid"), P(("tok", "dmod"), "hid")),
        check_vma=False,
    )
```

time: 463 us -> 104 us (0.22)
  waiting for transfers between devices: 340 us -> 0 us
  Pallas kernels: 0 us -> 98 us
  blocking collectives: 91 us -> 0 us
  between operations: 13.8 us -> 0.68 us
  matrix products: 10.5 us -> 0 us
    reduce_scatter x3 -> x0, waiting for transfers between devices: 208 us -> none  [the longest x1 79.8 us: shards(): lax.psum_scatter(partial_inputs, 'hid', scatter_dimension=0, tiled=True)]
    unnamed x7 -> x0, waiting for transfers between devices: 133 us -> none
    pallas_call x0 -> x1, Pallas kernels: none -> 98 us  [shards(): pl.pallas_call(functools.partial(kernel, ny, nz, cols), out_shape=(jax.Sh...]
    all_gather x4 -> x0, blocking collectives: 91 us -> none  [the longest x1 29.1 us: shards(): lax.all_gather(grad_gate, 'tok', axis=1, tiled=True)]
    dot_general x6 -> x0, matrix products: 10.5 us -> none  [the longest x1 2.84 us: shards(): up_part = jnp.dot(inputs, up_block, preferred_element_type=jnp.float32)]
  transfers between devices with their start and end apart: 5 -> 0, of which waited for: 5 -> 0; matrix products, arithmetic and copies ran while one was open for 2% -> 0% of each run, Pallas kernels for 0% -> 0%
where the time goes in v1:
time: 104 us
  Pallas kernels  98 us (94%)
  local copies, waits for them, and re-layouts  3.92 us (4%)
    pallas_call x1, Pallas kernels, shards(): pl.pallas_call(functools.partial(kernel, ny, nz, cols), out_shape=(jax.Sh...  98 us
    unnamed x9, local copies, waits for them, and re-layouts  3.92 us

profile of v1, /device:TPU:1, one launch (start us, length us, event | category | flops | bytes accessed | tf_op | source)
XLA Modules:
  0.0 103.5 jit_solution(11882234120426219193)
XLA Ops:
  0.6 0.0 copy-start.1
  0.7 1.0 bitcast_convert_fusion.gh_ref
  1.6 0.0 copy-done.1
  1.6 0.0 copy-start
  1.6 1.0 copy-done
  2.6 0.0 copy-start.2
  2.6 0.9 copy-done.2
  3.6 98.0 %step.1 = (bf16[24,512]{1,0:T(8,128)(2,1)S(1)}, bf16[128,896]{1,0:T(8,128)(2,1)S(1)}, bf16[128,896]{1,0:T(8,128)(2,1)S(1)}) custom-call(bf16[384,512]{1,0:T(8,128)(2,1)S(1)} %copy-done, f32[2,24,896]{2,1,0:T(8,128)S(1)} %bitcast_convert_fusion.gh_ref, bf16[128,896]{1,0:T(8,128)(2,1)S(1)} %copy-done.1, bf16[128,896]{1,0:T(8,128)(2,1)S(1)} %copy-done.2), custom_call_target="tpu_custom_call" | custom-call | tf_op jit(solution)/shard_map/step/pallas_call | solution.py:303
  101.5 0.6 copy.12
  102.2 0.7 copy.13
  102.8 0.7 copy.14
Async XLA Ops:
  0.6 1.0 copy-start.1
  1.6 1.0 copy-start
  2.6 0.9 copy-start.2

commit v2 on v1

v2 whole, which is shorter than its diff:
```python
import functools

import jax
import jax.numpy as jnp
from jax import lax
from jax.experimental import pallas as pl
from jax.experimental.pallas import tpu as pltpu
from jax.sharding import PartitionSpec as P

BF, F32 = jnp.bfloat16, jnp.float32
LANES = 128
GROUP = 4
SIGNS = (1, -1)


def contract(a, b, dims):
    return lax.dot_general(a, b, (dims, ((), ())), preferred_element_type=F32)


def widths(columns):
    tiles = columns // LANES
    return [2 * LANES] * (tiles // 2) + [LANES] * (tiles % 2)


def kernel(ny, nz, cols, x_ref, gh_ref, wg_ref, wu_ref, dx_ref, dwg_ref, dwu_ref, *scratch):
    n = len(cols)
    starts = [sum(cols[:i]) for i in range(n)]
    it = iter(scratch)
    take = lambda count: [next(it) for _ in range(count)]
    xs, xg, xt, ghw, zf, zs, ze, fx = take(8)
    z_far, z_near, z_anti, z_hub, z_hubs = take(5)
    wb, pb, pr, ys, gb, dwf, dws, dwr, dwh = (take(n) for _ in range(9))
    y_far, y_near, y_anti, y_hub, y_hubs = (take(n) for _ in range(5))
    in_s, x_s, x_r, t_s, t_r, gh_s, gh_r, f_s, f_r = take(9)
    w_s, w_r, p_s, p_r, ys_s, ys_r, g_s, g_r, k_s, k_r, d_s, d_r, zs_s, zs_r = take(14)

    tok, dmod, z = lax.axis_index("tok"), lax.axis_index("dmod"), lax.axis_index("hid")
    xl, y, xh, c = tok // ny, tok % ny, dmod // 2, dmod % 2
    other = 1 - c
    x = dmod - c + xl
    q = 2 * xl + xh
    tokens = x_ref.shape[0]
    share = tokens // (2 * ny)
    rows = tokens // nz
    home = c == xl

    def at(xl_=xl, xh_=xh, y_=y, c_=c, z_=z):
        return {"tok": xl_ * ny + y_, "dmod": xh_ * 2 + c_, "hid": z_}

    def along_x(k):
        xk = (x + 4 + k) % 4
        return 2 * (xk % 2) + xk // 2, at(xl_=xk % 2, xh_=xk // 2)

    def along(axis, k):
        if axis == "y":
            return (y + ny + k) % ny
        return (z + nz + k) % nz

    def there(axis, k):
        return at(y_=along("y", k)) if axis == "y" else at(z_=along("z", k))

    def send(src, dst, send_sem, recv_sem, target):
        copy = pltpu.make_async_remote_copy(
            src_ref=src, dst_ref=dst, send_sem=send_sem, recv_sem=recv_sem,
            device_id=target, device_id_type=pl.DeviceIdType.MESH,
        )
        copy.start()
        return copy

    def arrived(dst, sem):
        pltpu.make_async_copy(dst, dst, sem).wait()

    sent = arrived
    pending = []

    barrier = pltpu.get_barrier_semaphore()
    y_hops, z_hops = ny // 4, nz // 4
    y_off = sorted({s * k % ny for k in range(1, y_hops + 1) for s in SIGNS})
    z_off = sorted({s * k % nz for k in range(1, max(z_hops, GROUP - 1) + 1) for s in SIGNS} - {0})
    peers = [at(c_=other), at(xl_=1 - xl, c_=other)]
    peers += [along_x(k)[1] for k in (1, 2, 3)]
    peers += [there("y", k) for k in y_off] + [there("z", k) for k in z_off]
    for peer in peers:
        pl.semaphore_signal(barrier, 1, device_id=peer, device_id_type=pl.DeviceIdType.MESH)

    local = []

    def bring(src, dst):
        copy = pltpu.make_async_copy(src, dst, in_s.at[len(local)])
        copy.start()
        local.append(copy)

    for i in range(n):
        span = pl.ds(starts[i], cols[i])
        bring(wg_ref.at[:, span], wb[i].at[0, q])
        bring(wu_ref.at[:, span], wb[i].at[1, q])
    for h in range(2):
        for cc in range(2):
            bring(x_ref.at[:, pl.ds((2 * h + cc) * LANES, LANES)], xs.at[cc, h])

    def window(core):
        turn = core * ny + y
        first = pl.multiple_of(2 * share * (turn // 2) + 16 * (turn % 2), 16)
        return gh_ref.at[pl.ds(first, 32), :]

    own_gh = pltpu.make_async_copy(window(c), ghw, gh_r)

    @pl.when(home)
    def _():
        own_gh.start()

    for copy in local:
        copy.wait()

    @pl.when(home)
    def _():
        xg[xl] = xs[c]

    pl.semaphore_wait(barrier, len(peers))

    def weights_out(i):
        own = wb[i].at[:, q]
        for slot, k in enumerate(SIGNS):
            pending.append(send(own, own, w_s.at[i, slot], w_r.at[i, slot], along_x(k)[1]))

    part = tokens // GROUP
    turn = z % GROUP

    def part_of(slab, j):
        return slab.at[:, pl.ds(pl.multiple_of(j * part, part), part)]

    to_core = (xs.at[other], xg.at[xl], x_s.at[0], x_r.at[0], at(c_=other))
    to_gh = (window(other), ghw, gh_s, gh_r, at(c_=other))
    to_chip = [
        (part_of(xs.at[cc], turn), part_of(xg.at[xl], turn), x_s.at[cc], x_r.at[1],
         at(xl_=1 - xl, c_=cc))
        for cc in range(2)
    ]

    @pl.when(home)
    def _():
        send(*to_core)
        send(*to_gh)

    @pl.when(jnp.logical_not(home))
    def _():
        for args in to_chip:
            send(*args)

    weights_out(0)
    weights_out(1)

    def features():
        mine = part_of(xg.at[1 - xl], turn)
        arrived(mine, x_r.at[1])
        for k in range(1, GROUP):
            mate = z - turn + (turn + k) % GROUP
            pending.append(send(mine, mine, t_s.at[k - 1], t_r.at[k - 1], at(z_=mate)))

    def features_done():
        for k in range(1, GROUP):
            arrived(part_of(xg.at[1 - xl], (turn + GROUP - k) % GROUP), t_r.at[k - 1])

        @pl.when(jnp.logical_not(home))
        def _():
            arrived(xg.at[xl], x_r.at[0])

        for b in range(4):
            xt[b] = xg[b // 2, b % 2].astype(F32).T.astype(BF)

    def weights_on(i):
        for slot, k in enumerate(SIGNS):
            qk = along_x(-k)[0]
            arrived(wb[i].at[:, qk], w_r.at[i, slot])
            block = wb[i].at[slot, qk]
            pending.append(
                send(block, block, w_s.at[i, 2 + slot], w_r.at[i, 2 + slot], along_x(k)[1])
            )
        if i + 2 < n:
            weights_out(i + 2)

    def partial(i):
        qk = along_x(2)[0]
        for slot in range(2):
            arrived(wb[i].at[slot, qk], w_r.at[i, 2 + slot])
        wide = jnp.concatenate([xg[b // 2, b % 2] for b in range(4)], axis=1)
        for m in range(2):
            w = wb[i][m].reshape(4 * LANES, cols[i])
            block = contract(wide, w, ((1,), (0,))).reshape(2, ny, share, cols[i])
            pb[i][:, :, m * share : (m + 1) * share] = block
        pending.append(send(pb[i].at[other], pr[i], p_s.at[i], p_r.at[i], at(c_=other)))

    def reduce_start(axis, hops, src, far, near, anti, s_sem, r_sem):
        pick = lambda k: src.at[along(axis, k)]
        way = 2 * (along(axis, 0) % 2) - 1
        for j in range(hops - 1, 0, -1):
            for si, s in enumerate(SIGNS):
                slot = si * (hops - 1) + j - 1
                pending.append(
                    send(pick(s * (j + hops)), far.at[si, j - 1], s_sem.at[slot], r_sem.at[slot],
                         there(axis, s * j))
                )
        slot = 2 * (hops - 1)
        pending.append(
            send(pick(2 * hops), anti, s_sem.at[slot], r_sem.at[slot], there(axis, way * hops))
        )
        for j in range(1, hops):
            for si, s in enumerate(SIGNS):
                slot = (2 + si) * (hops - 1) + j
                pending.append(
                    send(pick(s * j), near.at[si, j - 1], s_sem.at[slot], r_sem.at[slot],
                         there(axis, s * j))
                )

    def reduce_relay(axis, hops, own, far, anti, hub, hubs, s_sem, r_sem):
        odd = along(axis, 0) % 2
        for j in range(1, hops):
            for si in range(2):
                arrived(far.at[si, j - 1], r_sem.at[si * (hops - 1) + j - 1])
        arrived(anti, r_sem.at[2 * (hops - 1)])
        for first in (True, False):
            si = 1 - odd if first else odd
            way = 1 - 2 * si
            total = own(along(axis, way * hops))
            for j in range(1, hops):
                total = total + far[si, j - 1].astype(F32)
            if first:
                total = total + anti[...].astype(F32)
            hubs[si] = total.astype(BF)
            slot = 4 * (hops - 1) + 1
            pending.append(
                send(hubs.at[si], hub.at[si], s_sem.at[slot + si], r_sem.at[slot + si],
                     there(axis, way * hops))
            )

    def reduce_end(axis, hops, own, near, hub, r_sem):
        total = own(along(axis, 0))
        for j in range(1, hops):
            for si in range(2):
                arrived(near.at[si, j - 1], r_sem.at[(2 + si) * (hops - 1) + j])
                total = total + near[si, j - 1].astype(F32)
        for si in range(2):
            arrived(hub.at[si], r_sem.at[4 * (hops - 1) + 1 + si])
            total = total + hub[si].astype(F32)
        return total

    def own_sum(i):
        return lambda yk: pb[i][c, yk] + pr[i][yk]

    def scatter(i):
        arrived(pr[i], p_r.at[i])
        ys[i][...] = (pb[i][c] + pr[i][...]).astype(BF)
        reduce_start("y", y_hops, ys[i], y_far[i], y_near[i], y_anti[i], ys_s.at[i], ys_r.at[i])

    def relay(i):
        reduce_relay("y", y_hops, own_sum(i), y_far[i], y_anti[i], y_hub[i], y_hubs[i],
                     ys_s.at[i], ys_r.at[i])

    def activate(i):
        if i == 0:
            @pl.when(home)
            def _():
                own_gh.wait()

            @pl.when(jnp.logical_not(home))
            def _():
                arrived(ghw, gh_r)

        total = reduce_end("y", y_hops, own_sum(i), y_near[i], y_hub[i], ys_r.at[i])
        gate, up = total[:share], total[share:]
        upstream = ghw[:, starts[i] : starts[i] + cols[i]].astype(F32)
        upstream = jnp.where((c * ny + y) % 2 == 1, upstream[8 : 8 + share], upstream[:share])
        sigma = jax.nn.sigmoid(gate)
        grad_gate = upstream * up * sigma * (1.0 + gate * (1.0 - sigma))
        grad_up = upstream * gate * sigma
        gb[i][c, y] = jnp.concatenate([grad_gate, grad_up], axis=0).astype(BF)
        own = gb[i].at[c, y]
        for k in range(y_hops, 0, -1):
            for s in SIGNS:
                slot = s * k % ny - 1
                pending.append(send(own, own, g_s.at[i, slot], g_r.at[i, slot], there("y", s * k)))

    def spread(i):
        for s in SIGNS:
            block = gb[i].at[c, along("y", -s * y_hops)]
            arrived(block, g_r.at[i, s * y_hops % ny - 1])
            for j in range(1, y_hops):
                slot = s * (j + y_hops) % ny - 1
                pending.append(send(block, block, g_s.at[i, slot], g_r.at[i, slot], there("y", s * j)))
        way = 2 * (y % 2) - 1
        block = gb[i].at[c, along("y", -way * y_hops)]
        slot = 2 * y_hops - 1
        pending.append(
            send(block, block, g_s.at[i, slot], g_r.at[i, slot], there("y", way * y_hops))
        )

    def gather(i):
        for k in range(1, ny):
            if k not in (y_hops, ny - y_hops):
                arrived(gb[i].at[c, along("y", -k)], g_r.at[i, k - 1])
        pending.append(send(gb[i].at[c], gb[i].at[c], k_s.at[i], k_r.at[i], at(c_=other)))

    def grads_of(i):
        both = gb[i][...].astype(F32).reshape(2 * ny, 2 * share, cols[i])
        grad_gate = both[:, :share].reshape(tokens, cols[i]).astype(BF)
        grad_up = both[:, share:].reshape(tokens, cols[i]).astype(BF)
        return grad_gate, grad_up

    def input_part(i):
        arrived(gb[i].at[other], k_r.at[i])
        grads = grads_of(i)
        for b in range(4):
            total = 0.0
            for m, grad in enumerate(grads):
                total = total + contract(grad, wb[i][m, b], ((1,), (1,)))
            total = total.reshape(nz, rows, LANES)
            span = slice(b * rows, (b + 1) * rows)
            zf[:, span] = total if i == 0 else zf[:, span] + total

    def weight_part(i):
        for m, grad in enumerate(grads_of(i)):
            for b in range(4):
                dwf[i][b, m] = contract(xt[b], grad, ((1,), (0,)))
        dws[i][...] = dwf[i][...].astype(BF)
        q2 = along_x(2)[0]
        for m, k in enumerate(SIGNS):
            pending.append(
                send(dws[i].at[q2, m], dwr[i].at[m], d_s.at[i, m], d_r.at[i, m], along_x(k)[1])
            )
        for m, k in enumerate(SIGNS):
            qk, target = along_x(k)
            pending.append(
                send(dws[i].at[qk, 1 - m], dwr[i].at[2 + m], d_s.at[i, 2 + m], d_r.at[i, 2 + m], target)
            )

    def weight_relay(i):
        for m, k in enumerate(SIGNS):
            qk, target = along_x(k)
            arrived(dwr[i].at[m], d_r.at[i, m])
            dwh[i][m] = (dwf[i][qk, m] + dwr[i][m].astype(F32)).astype(BF)
            pending.append(
                send(dwh[i].at[m], dwr[i].at[4 + m], d_s.at[i, 4 + m], d_r.at[i, 4 + m], target)
            )

    def weight_out(i):
        span = slice(starts[i], starts[i] + cols[i])
        for m, out in enumerate((dwg_ref, dwu_ref)):
            total = dwf[i][q, m]
            for slot in (3 - m, 4 + m):
                arrived(dwr[i].at[slot], d_r.at[i, slot])
                total = total + dwr[i][slot].astype(F32)
            out[:, span] = total.astype(BF)

    own_input = lambda zk: zf[zk]

    def input_start():
        zs[...] = zf[...].astype(BF)
        reduce_start("z", z_hops, zs, z_far, z_near, z_anti, zs_s, zs_r)

    def input_relay():
        reduce_relay("z", z_hops, own_input, z_far, z_anti, z_hub, z_hubs, zs_s, zs_r)

    ready = {
        weights_on: (6, 9, 13, 16),
        partial: (10, 14, 17, 18),
        scatter: (12, 16.2, 19, 20),
        relay: (16, 20, 23, 24),
        activate: (20, 24, 27, 28),
        spread: (24.5, 29, 31.5, 32.5),
        gather: (28, 32.4, 35, 36),
        input_part: (29, 33, 36.5, 37),
        weight_part: (29.5, 33.5, 38, 38.1),
        weight_relay: (34.4, 38.2, 43, 44),
        weight_out: (40, 42, 48, 49),
    }
    late = {features: 5, features_done: 9.9, input_start: 37.1, input_relay: 45}
    order = [(when, stage, None) for stage, when in late.items()]
    for stage, times in ready.items():
        shift = len(times) - n
        order += [(times[i if i < n - 1 else i + shift], stage, i) for i in range(n)]
    for _, stage, i in sorted(order, key=lambda entry: entry[0]):
        stage() if i is None else stage(i)

    half = 2 * rows
    total = reduce_end("z", z_hops, own_input, z_near, z_hub, zs_r)
    ze[...] = total.astype(BF).reshape(2, half, LANES)
    last = send(ze.at[1 - xl], fx.at[c], f_s.at[0], f_r.at[c], at(xl_=1 - xl, c_=xl))

    @pl.when(home)
    def _():
        fx[c] = ze[xl]

    @pl.when(jnp.logical_not(home))
    def _():
        send(ze.at[xl], fx.at[c], f_s.at[1], f_r.at[c], at(c_=other))
        arrived(fx.at[c], f_r.at[c])

    arrived(fx.at[other], f_r.at[other])
    for cc in range(2):
        got = fx[cc].astype(F32)
        for h in range(2):
            at_col = (2 * h + cc) * LANES
            dx_ref[:, at_col : at_col + LANES] = got[h * rows : (h + 1) * rows].astype(BF)

    @pl.when(home)
    def _():
        sent(xs.at[other], x_s.at[0])
        sent(window(other), gh_s)

    @pl.when(jnp.logical_not(home))
    def _():
        for cc in range(2):
            sent(part_of(xs.at[cc], turn), x_s.at[cc])
        sent(ze.at[xl], f_s.at[1])

    last.wait_send()
    for copy in pending:
        copy.wait_send()


def shards(ny, nz, inputs, grad_hidden, gate_weight, up_weight):
    tokens, features = inputs.shape
    columns = gate_weight.shape[1]
    cols = widths(columns)
    n = len(cols)
    share, rows = tokens // (2 * ny), tokens // nz
    yh, zh = ny // 4, nz // 4

    vmem = lambda shape, dtype=BF: pltpu.VMEM(shape, dtype)

    def ring(hops, block):
        return [
            (2, max(hops - 1, 1)) + block,
            (2, max(hops - 1, 1)) + block,
            block,
            (2,) + block,
            (2,) + block,
        ]

    z_block = (4 * rows, LANES)
    scratch = [
        vmem((2, 2, tokens, LANES)),
        vmem((2, 2, tokens, LANES)),
        vmem((4, LANES, tokens)),
        vmem((32, columns)),
        vmem((nz,) + z_block, F32),
        vmem((nz,) + z_block),
        vmem((2, 2 * rows, LANES)),
        vmem((2, 2 * rows, LANES)),
    ]
    scratch += [vmem(shape) for shape in ring(zh, z_block)]
    for shape, dtype in (
        (lambda w: (2, 4, LANES, w), BF),
        (lambda w: (2, ny, 2 * share, w), F32),
        (lambda w: (ny, 2 * share, w), F32),
        (lambda w: (ny, 2 * share, w), BF),
        (lambda w: (2, ny, 2 * share, w), BF),
        (lambda w: (4, 2, LANES, w), F32),
        (lambda w: (4, 2, LANES, w), BF),
        (lambda w: (6, LANES, w), BF),
        (lambda w: (2, LANES, w), BF),
    ):
        scratch += [vmem(shape(w), dtype) for w in cols]
    for j in range(5):
        scratch += [vmem(ring(yh, (2 * share, w))[j]) for w in cols]
    dma = pltpu.SemaphoreType.DMA
    scratch += [dma((2 * n + 4,)), dma((2,)), dma((2,)), dma((GROUP - 1,)), dma((GROUP - 1,))]
    scratch += [dma, dma, dma((2,)), dma((2,))]
    for shape in ((n, 4), (n,), (n, 4 * yh - 1), (n, ny - 1), (n,), (n, 6), (4 * zh - 1,)):
        scratch += [dma(shape), dma(shape)]

    in_hbm = pl.BlockSpec(memory_space=pl.ANY)
    in_vmem = pl.BlockSpec(memory_space=pltpu.VMEM)
    return pl.pallas_call(
        functools.partial(kernel, ny, nz, cols),
        out_shape=(
            jax.ShapeDtypeStruct((rows, features), BF),
            jax.ShapeDtypeStruct(gate_weight.shape, BF),
            jax.ShapeDtypeStruct(up_weight.shape, BF),
        ),
        in_specs=[in_hbm] * 4,
        out_specs=(in_vmem,) * 3,
        scratch_shapes=scratch,
        compiler_params=pltpu.CompilerParams(
            collective_id=0, has_side_effects=True, vmem_limit_bytes=36 * 2**20
        ),
        name="step",
    )(inputs, grad_hidden, gate_weight, up_weight)


def solution(mesh):
    placed = (
        P("dmod", "tok"),
        P("dmod", "hid"),
        P(("tok", "dmod"), "hid"),
        P(("tok", "dmod"), "hid"),
    )
    return jax.shard_map(
        functools.partial(shards, mesh.shape["tok"] // 2, mesh.shape["hid"]),
        mesh=mesh,
        in_specs=placed,
        out_specs=(P(("dmod", "hid"), "tok"), P(("tok", "dmod"), "hid"), P(("tok", "dmod"), "hid")),
        check_vma=False,
    )
```

time: 104 us -> 88.2 us (0.85)
  Pallas kernels: 98 us -> 81.3 us
  local copies, waits for them, and re-layouts: 3.92 us -> 5.95 us
    pallas_call x1, Pallas kernels: 98 us -> 81.3 us  [shards(): pl.pallas_call(functools.partial(kernel, ny, nz, cols), out_shape=(jax.Sh...]
    unnamed x9 -> x11, local copies, waits for them, and re-layouts: 3.92 us -> 5.95 us
where the time goes in v2:
time: 88.2 us; the launch traced here: 87.9 us
  Pallas kernels  81.3 us (92%)
  local copies, waits for them, and re-layouts  5.95 us (7%)
    pallas_call x1, Pallas kernels, shards(): pl.pallas_call(functools.partial(kernel, ny, nz, cols), out_shape=(jax.Sh...  81.3 us
    unnamed x11, local copies, waits for them, and re-layouts  5.95 us

profile of v2, /device:TPU:1, one launch (start us, length us, event | category | flops | bytes accessed | tf_op | source)
XLA Modules:
  0.0 87.9 jit_solution(17093673577872021575)
XLA Ops:
  0.6 0.0 copy-start
  0.6 1.1 %copy-done = bf16[384,896]{1,0:T(8,128)(2,1)S(1)} copy-done((bf16[384,896]{1,0:T(8,128)(2,1)S(1)}, bf16[384,896]{1,0:T(8,128)(2,1)}, u32[]{:S(2)}) %copy-start) | copy-done | bytes 688152
  1.7 0.0 copy-start.1
  1.7 1.0 %copy-done.1 = bf16[384,512]{1,0:T(8,128)(2,1)S(1)} copy-done((bf16[384,512]{1,0:T(8,128)(2,1)S(1)}, bf16[384,512]{1,0:T(8,128)(2,1)}, u32[]{:S(2)}) %copy-start.1) | copy-done | bytes 393240
  2.7 0.0 copy-start.2
  2.7 0.9 %copy-done.2 = bf16[128,896]{1,0:T(8,128)(2,1)S(1)} copy-done((bf16[128,896]{1,0:T(8,128)(2,1)S(1)}, bf16[128,896]{1,0:T(8,128)(2,1)}, u32[]{:S(2)}) %copy-start.2) | copy-done | bytes 229400
  3.7 0.0 copy-start.3
  3.7 0.9 %copy-done.3 = bf16[128,896]{1,0:T(8,128)(2,1)S(1)} copy-done((bf16[128,896]{1,0:T(8,128)(2,1)S(1)}, bf16[128,896]{1,0:T(8,128)(2,1)}, u32[]{:S(2)}) %copy-start.3) | copy-done | bytes 229400
  4.6 81.3 %step.1 = (bf16[24,512]{1,0:T(8,128)(2,1)S(1)}, bf16[128,896]{1,0:T(8,128)(2,1)S(1)}, bf16[128,896]{1,0:T(8,128)(2,1)S(1)}) custom-call(bf16[384,512]{1,0:T(8,128)(2,1)S(1)} %copy-done.1, bf16[384,896]{1,0:T(8,128)(2,1)S(1)} %copy-done, bf16[128,896]{1,0:T(8,128)(2,1)S(1)} %copy-done.2, bf16[128,896]{1,0:T(8,128)(2,1)S(1)} %copy-done.3), custom_call_target="tpu_custom_call" | custom-call | tf_op jit(solution)/shard_map/step/pallas_call | solution.py:474
  85.9 0.6 copy.10
  86.5 0.7 copy.11
  87.2 0.7 copy.12
Async XLA Ops:
  0.6 1.1 %copy-start = (bf16[384,896]{1,0:T(8,128)(2,1)S(1)}, bf16[384,896]{1,0:T(8,128)(2,1)}, u32[]{:S(2)}) copy-start(bf16[384,896]{1,0:T(8,128)(2,1)} %gh_ref.1) | copy-start | bytes 2064388
  1.7 1.0 %copy-start.1 = (bf16[384,512]{1,0:T(8,128)(2,1)S(1)}, bf16[384,512]{1,0:T(8,128)(2,1)}, u32[]{:S(2)}) copy-start(bf16[384,512]{1,0:T(8,128)(2,1)} %x_ref.1) | copy-start | bytes 1179652
  2.7 0.9 %copy-start.2 = (bf16[128,896]{1,0:T(8,128)(2,1)S(1)}, bf16[128,896]{1,0:T(8,128)(2,1)}, u32[]{:S(2)}) copy-start(bf16[128,896]{1,0:T(8,128)(2,1)} %wg_ref.1) | copy-start | bytes 688132
  3.7 0.9 %copy-start.3 = (bf16[128,896]{1,0:T(8,128)(2,1)S(1)}, bf16[128,896]{1,0:T(8,128)(2,1)}, u32[]{:S(2)}) copy-start(bf16[128,896]{1,0:T(8,128)(2,1)} %wu_ref.1) | copy-start | bytes 688132

commit v3 on v2

--- a/solution.py
+++ b/solution.py
@@ -32,7 +32,7 @@
     wb, pb, pr, ys, gb, dwf, dws, dwr, dwh = (take(n) for _ in range(9))
     y_far, y_near, y_anti, y_hub, y_hubs = (take(n) for _ in range(5))
     in_s, x_s, x_r, t_s, t_r, gh_s, gh_r, f_s, f_r = take(9)
-    w_s, w_r, p_s, p_r, ys_s, ys_r, g_s, g_r, k_s, k_r, d_s, d_r, zs_s, zs_r = take(14)
+    w_s, w_r, p_s, p_r, ys_s, ys_r, g_s, g_r, k_s, k_r, d_s, d_r, zs_s, zs_r, e_s, e_r = take(16)
 
     tok, dmod, z = lax.axis_index("tok"), lax.axis_index("dmod"), lax.axis_index("hid")
     xl, y, xh, c = tok // ny, tok % ny, dmod // 2, dmod % 2
@@ -80,6 +80,9 @@
     peers = [at(c_=other), at(xl_=1 - xl, c_=other)]
     peers += [along_x(k)[1] for k in (1, 2, 3)]
     peers += [there("y", k) for k in y_off] + [there("z", k) for k in z_off]
+    for k in sorted({s * z_hops % nz for s in SIGNS}):
+        for a, b in ((xl, other), (1 - xl, c), (1 - xl, other)):
+            peers.append(at(xl_=a, c_=b, z_=along("z", k)))
     for peer in peers:
         pl.semaphore_signal(barrier, 1, device_id=peer, device_id_type=pl.DeviceIdType.MESH)
 
@@ -212,7 +215,7 @@
                          there(axis, s * j))
                 )
 
-    def reduce_relay(axis, hops, own, far, anti, hub, hubs, s_sem, r_sem):
+    def reduce_relay(axis, hops, own, far, anti, hubs, r_sem, deliver):
         odd = along(axis, 0) % 2
         for j in range(1, hops):
             for si in range(2):
@@ -227,21 +230,14 @@
             if first:
                 total = total + anti[...].astype(F32)
             hubs[si] = total.astype(BF)
-            slot = 4 * (hops - 1) + 1
-            pending.append(
-                send(hubs.at[si], hub.at[si], s_sem.at[slot + si], r_sem.at[slot + si],
-                     there(axis, way * hops))
-            )
-
-    def reduce_end(axis, hops, own, near, hub, r_sem):
+            deliver(si, along(axis, way * hops))
+
+    def reduce_near(axis, hops, own, near, r_sem):
         total = own(along(axis, 0))
         for j in range(1, hops):
             for si in range(2):
                 arrived(near.at[si, j - 1], r_sem.at[(2 + si) * (hops - 1) + j])
                 total = total + near[si, j - 1].astype(F32)
-        for si in range(2):
-            arrived(hub.at[si], r_sem.at[4 * (hops - 1) + 1 + si])
-            total = total + hub[si].astype(F32)
         return total
 
     def own_sum(i):
@@ -252,9 +248,16 @@
         ys[i][...] = (pb[i][c] + pr[i][...]).astype(BF)
         reduce_start("y", y_hops, ys[i], y_far[i], y_near[i], y_anti[i], ys_s.at[i], ys_r.at[i])
 
+    y_slot = 4 * (y_hops - 1) + 1
+
     def relay(i):
-        reduce_relay("y", y_hops, own_sum(i), y_far[i], y_anti[i], y_hub[i], y_hubs[i],
-                     ys_s.at[i], ys_r.at[i])
+        def deliver(si, yk):
+            src, slot = y_hubs[i].at[si], y_slot + si
+            pending.append(
+                send(src, y_hub[i].at[si], ys_s.at[i, slot], ys_r.at[i, slot], at(y_=yk))
+            )
+
+        reduce_relay("y", y_hops, own_sum(i), y_far[i], y_anti[i], y_hubs[i], ys_r.at[i], deliver)
 
     def activate(i):
         if i == 0:
@@ -266,7 +269,10 @@
             def _():
                 arrived(ghw, gh_r)
 
-        total = reduce_end("y", y_hops, own_sum(i), y_near[i], y_hub[i], ys_r.at[i])
+        total = reduce_near("y", y_hops, own_sum(i), y_near[i], ys_r.at[i])
+        for si in range(2):
+            arrived(y_hub[i].at[si], ys_r.at[i, y_slot + si])
+            total = total + y_hub[i][si].astype(F32)
         gate, up = total[:share], total[share:]
         upstream = ghw[:, starts[i] : starts[i] + cols[i]].astype(F32)
         upstream = jnp.where((c * ny + y) % 2 == 1, upstream[8 : 8 + share], upstream[:share])
@@ -357,23 +363,45 @@
         zs[...] = zf[...].astype(BF)
         reduce_start("z", z_hops, zs, z_far, z_near, z_anti, zs_s, zs_r)
 
+    half = 2 * rows
+
     def input_relay():
-        reduce_relay("z", z_hops, own_input, z_far, z_anti, z_hub, z_hubs, zs_s, zs_r)
+        def deliver(si, zk):
+            for to in range(2):
+                target = at(xl_=to, c_=xl, z_=zk)
+                src = z_hubs.at[si, pl.ds(to * half, half)]
+                pending.append(send(src, z_hub.at[si, c], e_s.at[si, to], e_r.at[si, c], target))
+
+        reduce_relay("z", z_hops, own_input, z_far, z_anti, z_hubs, zs_r, deliver)
+
+    def input_near():
+        total = reduce_near("z", z_hops, own_input, z_near, zs_r)
+        ze[...] = total.reshape(2, half, LANES)
+        target = at(xl_=1 - xl, c_=xl)
+        pending.append(send(ze.at[1 - xl], fx.at[c], f_s.at[0], f_r.at[c], target))
+
+        @pl.when(home)
+        def _():
+            fx[c] = ze[xl]
+
+        @pl.when(jnp.logical_not(home))
+        def _():
+            send(ze.at[xl], fx.at[c], f_s.at[1], f_r.at[c], at(c_=other))
 
     ready = {
-        weights_on: (6, 9, 13, 16),
-        partial: (10, 14, 17, 18),
-        scatter: (12, 16.2, 19, 20),
-        relay: (16, 20, 23, 24),
-        activate: (20, 24, 27, 28),
-        spread: (24.5, 29, 31.5, 32.5),
-        gather: (28, 32.4, 35, 36),
-        input_part: (29, 33, 36.5, 37),
-        weight_part: (29.5, 33.5, 38, 38.1),
-        weight_relay: (34.4, 38.2, 43, 44),
-        weight_out: (40, 42, 48, 49),
+        weights_on: (9, 11.8, 18.2, 20.3),
+        partial: (14.7, 18.7, 22.5, 23.1),
+        scatter: (16.2, 22.2, 24.6, 26.1),
+        relay: (21.5, 26.4, 27.3, 30.3),
+        activate: (25.2, 31.7, 32.9, 35),
+        spread: (29.2, 36.6, 37.4, 38.1),
+        gather: (34, 39.3, 41.2, 43),
+        input_part: (35.6, 42, 43.2, 44.3),
+        weight_part: (36.8, 42.4, 43.6, 45.1),
+        weight_relay: (40.7, 45.7, 46.8, 49.6),
+        weight_out: (45.5, 55, 56, 57),
     }
-    late = {features: 5, features_done: 9.9, input_start: 37.1, input_relay: 45}
+    late = {features: 5, features_done: 14.6, input_start: 44.5, input_relay: 51.6, input_near: 53}
     order = [(when, stage, None) for stage, when in late.items()]
     for stage, times in ready.items():
         shift = len(times) - n
@@ -381,23 +409,16 @@
     for _, stage, i in sorted(order, key=lambda entry: entry[0]):
         stage() if i is None else stage(i)
 
-    half = 2 * rows
-    total = reduce_end("z", z_hops, own_input, z_near, z_hub, zs_r)
-    ze[...] = total.astype(BF).reshape(2, half, LANES)
-    last = send(ze.at[1 - xl], fx.at[c], f_s.at[0], f_r.at[c], at(xl_=1 - xl, c_=xl))
-
-    @pl.when(home)
-    def _():
-        fx[c] = ze[xl]
-
     @pl.when(jnp.logical_not(home))
     def _():
-        send(ze.at[xl], fx.at[c], f_s.at[1], f_r.at[c], at(c_=other))
         arrived(fx.at[c], f_r.at[c])
 
     arrived(fx.at[other], f_r.at[other])
+    for si in range(2):
+        for cc in range(2):
+            arrived(z_hub.at[si, cc], e_r.at[si, cc])
     for cc in range(2):
-        got = fx[cc].astype(F32)
+        got = fx[cc] + z_hub[0, cc].astype(F32) + z_hub[1, cc].astype(F32)
         for h in range(2):
             at_col = (2 * h + cc) * LANES
             dx_ref[:, at_col : at_col + LANES] = got[h * rows : (h + 1) * rows].astype(BF)
@@ -413,9 +434,17 @@
             sent(part_of(xs.at[cc], turn), x_s.at[cc])
         sent(ze.at[xl], f_s.at[1])
 
-    last.wait_send()
     for copy in pending:
         copy.wait_send()
+
+
+def store(a_ref, b_ref, c_ref, a_out, b_out, c_out, sem):
+    pairs = ((a_ref, a_out), (b_ref, b_out), (c_ref, c_out))
+    copies = [pltpu.make_async_copy(src, dst, sem.at[i]) for i, (src, dst) in enumerate(pairs)]
+    for copy in copies:
+        copy.start()
+    for copy in copies:
+        copy.wait()
 
 
 def shards(ny, nz, inputs, grad_hidden, gate_weight, up_weight):
@@ -445,10 +474,12 @@
         vmem((32, columns)),
         vmem((nz,) + z_block, F32),
         vmem((nz,) + z_block),
-        vmem((2, 2 * rows, LANES)),
-        vmem((2, 2 * rows, LANES)),
+        vmem((2, 2 * rows, LANES), F32),
+        vmem((2, 2 * rows, LANES), F32),
     ]
-    scratch += [vmem(shape) for shape in ring(zh, z_block)]
+    z_ring = ring(zh, z_block)
+    z_ring[3] = (2, 2, 2 * rows, LANES)
+    scratch += [vmem(shape) for shape in z_ring]
     for shape, dtype in (
         (lambda w: (2, 4, LANES, w), BF),
         (lambda w: (2, ny, 2 * share, w), F32),
@@ -468,10 +499,12 @@
     scratch += [dma, dma, dma((2,)), dma((2,))]
     for shape in ((n, 4), (n,), (n, 4 * yh - 1), (n, ny - 1), (n,), (n, 6), (4 * zh - 1,)):
         scratch += [dma(shape), dma(shape)]
-
+    scratch += [dma((2, 2)), dma((2, 2))]
+
+    arrays = (inputs, grad_hidden, gate_weight, up_weight)
     in_hbm = pl.BlockSpec(memory_space=pl.ANY)
     in_vmem = pl.BlockSpec(memory_space=pltpu.VMEM)
-    return pl.pallas_call(
+    results = pl.pallas_call(
         functools.partial(kernel, ny, nz, cols),
         out_shape=(
             jax.ShapeDtypeStruct((rows, features), BF),
@@ -485,7 +518,15 @@
             collective_id=0, has_side_effects=True, vmem_limit_bytes=36 * 2**20
         ),
         name="step",
-    )(inputs, grad_hidden, gate_weight, up_weight)
+    )(*(pltpu.with_memory_space_constraint(a, pltpu.HBM) for a in arrays))
+    return pl.pallas_call(
+        store,
+        out_shape=tuple(jax.ShapeDtypeStruct(r.shape, r.dtype) for r in results),
+        in_specs=[pl.BlockSpec(memory_space=pl.ANY)] * 3,
+        out_specs=(pl.BlockSpec(memory_space=pl.ANY),) * 3,
+        scratch_shapes=[dma((3,))],
+        name="store",
+    )(*results)
 
 
 def solution(mesh):

time: 88.2 us -> 96.5 us (1.094)
  Pallas kernels: 81.3 us -> 93.7 us
  local copies, waits for them, and re-layouts: 5.95 us -> 1.96 us
    pallas_call x0 -> x1, Pallas kernels: none -> 15.8 us  [shards(): pl.pallas_call(store, out_shape=tuple((jax.ShapeDtypeStruct(r.shape, r.dt...]
    unnamed x11 -> x6, local copies, waits for them, and re-layouts: 5.95 us -> 1.96 us
    pallas_call x1, Pallas kernels: 81.3 us -> 77.9 us  [shards(): pl.pallas_call(functools.partial(kernel, ny, nz, cols), out_shape=(jax.Sh...]
where the time goes in v3:
time: 96.5 us; the launch traced here: 96.3 us
  Pallas kernels  93.7 us (97%)
  local copies, waits for them, and re-layouts  1.96 us (2%)
    pallas_call x1, Pallas kernels, shards(): pl.pallas_call(functools.partial(kernel, ny, nz, cols), out_shape=(jax.Sh...  77.9 us
    pallas_call x1, Pallas kernels, shards(): pl.pallas_call(store, out_shape=tuple((jax.ShapeDtypeStruct(r.shape, r.dt...  15.8 us
    unnamed x6, local copies, waits for them, and re-layouts  1.96 us

profile of v3, /device:TPU:1, one launch (start us, length us, event | category | flops | bytes accessed | tf_op | source)
XLA Modules:
  0.0 96.3 jit_solution(7855742038682257138)
XLA Ops:
  0.6 77.9 %step.1 = (bf16[24,512]{1,0:T(8,128)(2,1)S(1)}, bf16[128,896]{1,0:T(8,128)(2,1)S(1)}, bf16[128,896]{1,0:T(8,128)(2,1)S(1)}) custom-call(bf16[384,512]{1,0:T(8,128)(2,1)} %x_ref.1, bf16[384,896]{1,0:T(8,128)(2,1)} %gh_ref.1, bf16[128,896]{1,0:T(8,128)(2,1)} %wg_ref.1, bf16[128,896]{1,0:T(8,128)(2,1)} %wu_ref.1), custom_call_target="tpu_custom_call" | custom-call | tf_op jit(solution)/shard_map/step/pallas_call | solution.py:507
  78.6 0.0 copy-start
  78.6 0.7 copy-done
  79.3 0.0 copy-start.1
  79.3 0.7 copy-done.1
  79.9 0.0 copy-start.2
  79.9 0.6 copy-done.2
  80.5 15.8 %store.1 = (bf16[24,512]{1,0:T(8,128)(2,1)}, bf16[128,896]{1,0:T(8,128)(2,1)}, bf16[128,896]{1,0:T(8,128)(2,1)}) custom-call(bf16[24,512]{1,0:T(8,128)(2,1)} %copy-done.2, bf16[128,896]{1,0:T(8,128)(2,1)} %copy-done, bf16[128,896]{1,0:T(8,128)(2,1)} %copy-done.1), custom_call_target="tpu_custom_call" | custom-call | tf_op jit(solution)/shard_map/store/pallas_call | solution.py:522
Async XLA Ops:
  78.6 0.7 copy-start
  79.3 0.7 copy-start.1
  79.9 0.6 copy-start.2

commit v4 on v3

--- a/solution.py
+++ b/solution.py
@@ -77,13 +77,12 @@
     y_hops, z_hops = ny // 4, nz // 4
     y_off = sorted({s * k % ny for k in range(1, y_hops + 1) for s in SIGNS})
     z_off = sorted({s * k % nz for k in range(1, max(z_hops, GROUP - 1) + 1) for s in SIGNS} - {0})
-    peers = [at(c_=other), at(xl_=1 - xl, c_=other)]
-    peers += [along_x(k)[1] for k in (1, 2, 3)]
+    peers = [at(c_=other), at(xl_=1 - xl, c_=other)] + [along_x(k)[1] for k in SIGNS]
     peers += [there("y", k) for k in y_off] + [there("z", k) for k in z_off]
     for k in sorted({s * z_hops % nz for s in SIGNS}):
         for a, b in ((xl, other), (1 - xl, c), (1 - xl, other)):
             peers.append(at(xl_=a, c_=b, z_=along("z", k)))
-    for peer in peers:
+    for peer in peers[::-1]:
         pl.semaphore_signal(barrier, 1, device_id=peer, device_id_type=pl.DeviceIdType.MESH)
 
     local = []
@@ -436,15 +435,6 @@
 
     for copy in pending:
         copy.wait_send()
-
-
-def store(a_ref, b_ref, c_ref, a_out, b_out, c_out, sem):
-    pairs = ((a_ref, a_out), (b_ref, b_out), (c_ref, c_out))
-    copies = [pltpu.make_async_copy(src, dst, sem.at[i]) for i, (src, dst) in enumerate(pairs)]
-    for copy in copies:
-        copy.start()
-    for copy in copies:
-        copy.wait()
 
 
 def shards(ny, nz, inputs, grad_hidden, gate_weight, up_weight):
@@ -504,7 +494,7 @@
     arrays = (inputs, grad_hidden, gate_weight, up_weight)
     in_hbm = pl.BlockSpec(memory_space=pl.ANY)
     in_vmem = pl.BlockSpec(memory_space=pltpu.VMEM)
-    results = pl.pallas_call(
+    return pl.pallas_call(
         functools.partial(kernel, ny, nz, cols),
         out_shape=(
             jax.ShapeDtypeStruct((rows, features), BF),
@@ -519,14 +509,6 @@
         ),
         name="step",
     )(*(pltpu.with_memory_space_constraint(a, pltpu.HBM) for a in arrays))
-    return pl.pallas_call(
-        store,
-        out_shape=tuple(jax.ShapeDtypeStruct(r.shape, r.dtype) for r in results),
-        in_specs=[pl.BlockSpec(memory_space=pl.ANY)] * 3,
-        out_specs=(pl.BlockSpec(memory_space=pl.ANY),) * 3,
-        scratch_shapes=[dma((3,))],
-        name="store",
-    )(*results)
 
 
 def solution(mesh):

time: 96.5 us -> 80.5 us (0.83)
  Pallas kernels: 93.7 us -> 77.6 us
    pallas_call x1 -> x0, Pallas kernels: 15.8 us -> none  [shards(): pl.pallas_call(store, out_shape=tuple((jax.ShapeDtypeStruct(r.shape, r.dt...]
    unnamed x6 -> x3, local copies, waits for them, and re-layouts: 1.96 us -> 1.99 us
where the time goes in v4:
time: 80.5 us; the launch traced here: 80.3 us
  Pallas kernels  77.6 us (96%)
  local copies, waits for them, and re-layouts  1.99 us (2%)
    pallas_call x1, Pallas kernels, shards(): pl.pallas_call(functools.partial(kernel, ny, nz, cols), out_shape=(jax.Sh...  77.6 us
    unnamed x3, local copies, waits for them, and re-layouts  1.99 us

profile of v4, /device:TPU:1, one launch (start us, length us, event | category | flops | bytes accessed | tf_op | source)
XLA Modules:
  0.0 80.3 jit_solution(4981952388854570540)
XLA Ops:
  0.6 77.6 %step.1 = (bf16[24,512]{1,0:T(8,128)(2,1)S(1)}, bf16[128,896]{1,0:T(8,128)(2,1)S(1)}, bf16[128,896]{1,0:T(8,128)(2,1)S(1)}) custom-call(bf16[384,512]{1,0:T(8,128)(2,1)} %x_ref.1, bf16[384,896]{1,0:T(8,128)(2,1)} %gh_ref.1, bf16[128,896]{1,0:T(8,128)(2,1)} %wg_ref.1, bf16[128,896]{1,0:T(8,128)(2,1)} %wu_ref.1), custom_call_target="tpu_custom_call" | custom-call | tf_op jit(solution)/shard_map/step/pallas_call | solution.py:497
  78.3 0.6 copy.10
  78.9 0.7 copy.11
  79.6 0.7 copy.12

commit v5 on v4

--- a/solution.py
+++ b/solution.py
@@ -22,7 +22,7 @@
     return [2 * LANES] * (tiles // 2) + [LANES] * (tiles % 2)
 
 
-def kernel(ny, nz, cols, x_ref, gh_ref, wg_ref, wu_ref, dx_ref, dwg_ref, dwu_ref, *scratch):
+def kernel(ny, nz, cols, x_ref, gh_ref, wg_ref, wu_ref, dx_ref, dw_ref, *scratch):
     n = len(cols)
     starts = [sum(cols[:i]) for i in range(n)]
     it = iter(scratch)
@@ -82,9 +82,6 @@
     for k in sorted({s * z_hops % nz for s in SIGNS}):
         for a, b in ((xl, other), (1 - xl, c), (1 - xl, other)):
             peers.append(at(xl_=a, c_=b, z_=along("z", k)))
-    for peer in peers[::-1]:
-        pl.semaphore_signal(barrier, 1, device_id=peer, device_id_type=pl.DeviceIdType.MESH)
-
     local = []
 
     def bring(src, dst):
@@ -92,13 +89,20 @@
         copy.start()
         local.append(copy)
 
-    for i in range(n):
+    def bring_weights(i):
         span = pl.ds(starts[i], cols[i])
         bring(wg_ref.at[:, span], wb[i].at[0, q])
         bring(wu_ref.at[:, span], wb[i].at[1, q])
+
+    bring_weights(0)
     for h in range(2):
         for cc in range(2):
             bring(x_ref.at[:, pl.ds((2 * h + cc) * LANES, LANES)], xs.at[cc, h])
+    first_in = len(local)
+    for peer in peers[::-1]:
+        pl.semaphore_signal(barrier, 1, device_id=peer, device_id_type=pl.DeviceIdType.MESH)
+    for i in range(1, n):
+        bring_weights(i)
 
     def window(core):
         turn = core * ny + y
@@ -111,7 +115,7 @@
     def _():
         own_gh.start()
 
-    for copy in local:
+    for copy in local[:first_in]:
         copy.wait()
 
     @pl.when(home)
@@ -150,6 +154,8 @@
             send(*args)
 
     weights_out(0)
+    for copy in local[first_in:]:
+        copy.wait()
     weights_out(1)
 
     def features():
@@ -192,55 +198,63 @@
             pb[i][:, :, m * share : (m + 1) * share] = block
         pending.append(send(pb[i].at[other], pr[i], p_s.at[i], p_r.at[i], at(c_=other)))
 
-    def reduce_start(axis, hops, src, far, near, anti, s_sem, r_sem):
-        pick = lambda k: src.at[along(axis, k)]
+    def reduce_start(axis, hops, src, far, near, anti, s_sem, r_sem, cuts=1):
+        place = lambda k: along(axis, k)
         way = 2 * (along(axis, 0) % 2) - 1
-        for j in range(hops - 1, 0, -1):
+        lines = src.shape[1] // cuts
+        for cut in range(cuts):
+            part = pl.ds(cut * lines, lines)
+            for j in range(hops - 1, 0, -1):
+                for si, s in enumerate(SIGNS):
+                    slot = (si * (hops - 1) + j - 1) * cuts + cut
+                    pending.append(
+                        send(src.at[place(s * (j + hops)), part], far.at[si, j - 1, part],
+                             s_sem.at[slot], r_sem.at[slot], there(axis, s * j))
+                    )
+            slot = 2 * (hops - 1) * cuts + cut
+            pending.append(
+                send(src.at[place(2 * hops), part], anti.at[part], s_sem.at[slot], r_sem.at[slot],
+                     there(axis, way * hops))
+            )
+        for j in range(1, hops):
             for si, s in enumerate(SIGNS):
-                slot = si * (hops - 1) + j - 1
+                slot = (2 * hops - 1) * cuts + si * (hops - 1) + j - 1
                 pending.append(
-                    send(pick(s * (j + hops)), far.at[si, j - 1], s_sem.at[slot], r_sem.at[slot],
+                    send(src.at[place(s * j)], near.at[si, j - 1], s_sem.at[slot], r_sem.at[slot],
                          there(axis, s * j))
                 )
-        slot = 2 * (hops - 1)
-        pending.append(
-            send(pick(2 * hops), anti, s_sem.at[slot], r_sem.at[slot], there(axis, way * hops))
-        )
-        for j in range(1, hops):
-            for si, s in enumerate(SIGNS):
-                slot = (2 + si) * (hops - 1) + j
-                pending.append(
-                    send(pick(s * j), near.at[si, j - 1], s_sem.at[slot], r_sem.at[slot],
-                         there(axis, s * j))
-                )
-
-    def reduce_relay(axis, hops, own, far, anti, hubs, r_sem, deliver):
+
+    def reduce_relay(axis, hops, own, far, anti, hubs, r_sem, deliver, cut=0, cuts=1):
         odd = along(axis, 0) % 2
+        lines = hubs.shape[1] // cuts
+        part = pl.ds(cut * lines, lines)
         for j in range(1, hops):
             for si in range(2):
-                arrived(far.at[si, j - 1], r_sem.at[si * (hops - 1) + j - 1])
-        arrived(anti, r_sem.at[2 * (hops - 1)])
+                slot = (si * (hops - 1) + j - 1) * cuts + cut
+                arrived(far.at[si, j - 1, part], r_sem.at[slot])
+        arrived(anti.at[part], r_sem.at[2 * (hops - 1) * cuts + cut])
         for first in (True, False):
             si = 1 - odd if first else odd
             way = 1 - 2 * si
-            total = own(along(axis, way * hops))
+            total = own(along(axis, way * hops), part)
             for j in range(1, hops):
-                total = total + far[si, j - 1].astype(F32)
+                total = total + far[si, j - 1, part].astype(F32)
             if first:
-                total = total + anti[...].astype(F32)
-            hubs[si] = total.astype(BF)
+                total = total + anti[part].astype(F32)
+            hubs[si, part] = total.astype(BF)
             deliver(si, along(axis, way * hops))
 
-    def reduce_near(axis, hops, own, near, r_sem):
-        total = own(along(axis, 0))
+    def reduce_near(axis, hops, own, near, r_sem, cuts=1):
+        total = own(along(axis, 0), slice(None))
         for j in range(1, hops):
             for si in range(2):
-                arrived(near.at[si, j - 1], r_sem.at[(2 + si) * (hops - 1) + j])
+                slot = (2 * hops - 1) * cuts + si * (hops - 1) + j - 1
+                arrived(near.at[si, j - 1], r_sem.at[slot])
                 total = total + near[si, j - 1].astype(F32)
         return total
 
     def own_sum(i):
-        return lambda yk: pb[i][c, yk] + pr[i][yk]
+        return lambda yk, part: pb[i][c, yk, part] + pr[i][yk, part]
 
     def scatter(i):
         arrived(pr[i], p_r.at[i])
@@ -349,32 +363,31 @@
 
     def weight_out(i):
         span = slice(starts[i], starts[i] + cols[i])
-        for m, out in enumerate((dwg_ref, dwu_ref)):
+        for m in range(2):
             total = dwf[i][q, m]
             for slot in (3 - m, 4 + m):
                 arrived(dwr[i].at[slot], d_r.at[i, slot])
                 total = total + dwr[i][slot].astype(F32)
-            out[:, span] = total.astype(BF)
-
-    own_input = lambda zk: zf[zk]
+            dw_ref[m, :, span] = total.astype(BF)
+
+    own_input = lambda zk, part: zf[zk, part]
 
     def input_start():
         zs[...] = zf[...].astype(BF)
-        reduce_start("z", z_hops, zs, z_far, z_near, z_anti, zs_s, zs_r)
+        reduce_start("z", z_hops, zs, z_far, z_near, z_anti, zs_s, zs_r, 2)
 
     half = 2 * rows
 
-    def input_relay():
+    def input_relay(to):
         def deliver(si, zk):
-            for to in range(2):
-                target = at(xl_=to, c_=xl, z_=zk)
-                src = z_hubs.at[si, pl.ds(to * half, half)]
-                pending.append(send(src, z_hub.at[si, c], e_s.at[si, to], e_r.at[si, c], target))
-
-        reduce_relay("z", z_hops, own_input, z_far, z_anti, z_hubs, zs_r, deliver)
+            target = at(xl_=to, c_=xl, z_=zk)
+            src = z_hubs.at[si, pl.ds(to * half, half)]
+            pending.append(send(src, z_hub.at[si, c], e_s.at[si, to], e_r.at[si, c], target))
+
+        reduce_relay("z", z_hops, own_input, z_far, z_anti, z_hubs, zs_r, deliver, to, 2)
 
     def input_near():
-        total = reduce_near("z", z_hops, own_input, z_near, zs_r)
+        total = reduce_near("z", z_hops, own_input, z_near, zs_r, 2)
         ze[...] = total.reshape(2, half, LANES)
         target = at(xl_=1 - xl, c_=xl)
         pending.append(send(ze.at[1 - xl], fx.at[c], f_s.at[0], f_r.at[c], target))
@@ -400,13 +413,28 @@
         weight_relay: (40.7, 45.7, 46.8, 49.6),
         weight_out: (45.5, 55, 56, 57),
     }
-    late = {features: 5, features_done: 14.6, input_start: 44.5, input_relay: 51.6, input_near: 53}
+    late = {features: 5, features_done: 14.6, input_start: 44.5, input_near: 53}
     order = [(when, stage, None) for stage, when in late.items()]
+    order += [(48.5, input_relay, 0), (51.6, input_relay, 1)]
     for stage, times in ready.items():
         shift = len(times) - n
         order += [(times[i if i < n - 1 else i + shift], stage, i) for i in range(n)]
     for _, stage, i in sorted(order, key=lambda entry: entry[0]):
         stage() if i is None else stage(i)
+
+    recent = 24
+    for copy in pending[:-recent]:
+        copy.wait_send()
+
+    @pl.when(home)
+    def _():
+        sent(xs.at[other], x_s.at[0])
+        sent(window(other), gh_s)
+
+    @pl.when(jnp.logical_not(home))
+    def _():
+        for cc in range(2):
+            sent(part_of(xs.at[cc], turn), x_s.at[cc])
 
     @pl.when(jnp.logical_not(home))
     def _():
@@ -422,18 +450,11 @@
             at_col = (2 * h + cc) * LANES
             dx_ref[:, at_col : at_col + LANES] = got[h * rows : (h + 1) * rows].astype(BF)
 
-    @pl.when(home)
-    def _():
-        sent(xs.at[other], x_s.at[0])
-        sent(window(other), gh_s)
-
     @pl.when(jnp.logical_not(home))
     def _():
-        for cc in range(2):
-            sent(part_of(xs.at[cc], turn), x_s.at[cc])
         sent(ze.at[xl], f_s.at[1])
 
-    for copy in pending:
+    for copy in pending[-recent:]:
         copy.wait_send()
 
 
@@ -487,28 +508,28 @@
     dma = pltpu.SemaphoreType.DMA
     scratch += [dma((2 * n + 4,)), dma((2,)), dma((2,)), dma((GROUP - 1,)), dma((GROUP - 1,))]
     scratch += [dma, dma, dma((2,)), dma((2,))]
-    for shape in ((n, 4), (n,), (n, 4 * yh - 1), (n, ny - 1), (n,), (n, 6), (4 * zh - 1,)):
+    for shape in ((n, 4), (n,), (n, 4 * yh - 1), (n, ny - 1), (n,), (n, 6), (6 * zh - 4,)):
         scratch += [dma(shape), dma(shape)]
     scratch += [dma((2, 2)), dma((2, 2))]
 
     arrays = (inputs, grad_hidden, gate_weight, up_weight)
     in_hbm = pl.BlockSpec(memory_space=pl.ANY)
     in_vmem = pl.BlockSpec(memory_space=pltpu.VMEM)
-    return pl.pallas_call(
+    grad_inputs, grad_weights = pl.pallas_call(
         functools.partial(kernel, ny, nz, cols),
         out_shape=(
             jax.ShapeDtypeStruct((rows, features), BF),
-            jax.ShapeDtypeStruct(gate_weight.shape, BF),
-            jax.ShapeDtypeStruct(up_weight.shape, BF),
+            jax.ShapeDtypeStruct((2,) + gate_weight.shape, BF),
         ),
         in_specs=[in_hbm] * 4,
-        out_specs=(in_vmem,) * 3,
+        out_specs=(in_vmem,) * 2,
         scratch_shapes=scratch,
         compiler_params=pltpu.CompilerParams(
             collective_id=0, has_side_effects=True, vmem_limit_bytes=36 * 2**20
         ),
         name="step",
     )(*(pltpu.with_memory_space_constraint(a, pltpu.HBM) for a in arrays))
+    return grad_inputs, grad_weights[0], grad_weights[1]
 
 
 def solution(mesh):

time: 80.5 us -> 79.9 us (level)
    unnamed x3 -> x1, local copies, waits for them, and re-layouts: 1.99 us -> 0.61 us
where the time goes in v5:
time: 79.9 us; the launch traced here: 79.7 us
  Pallas kernels  77.7 us (97%)
  local copies, waits for them, and re-layouts  1.41 us (2%)
    pallas_call x1, Pallas kernels, shards(): pl.pallas_call(functools.partial(kernel, ny, nz, cols), out_shape=(jax.Sh...  77.7 us

profile of v5, /device:TPU:1, one launch (start us, length us, event | category | flops | bytes accessed | tf_op | source)
XLA Modules:
  0.0 79.7 jit_solution(6691559136736440863)
XLA Ops:
  0.6 77.7 %step.1 = (bf16[24,512]{1,0:T(8,128)(2,1)S(1)}, bf16[2,128,896]{2,1,0:T(8,128)(2,1)S(1)}) custom-call(bf16[384,512]{1,0:T(8,128)(2,1)} %x_ref.1, bf16[384,896]{1,0:T(8,128)(2,1)} %gh_ref.1, bf16[128,896]{1,0:T(8,128)(2,1)} %wg_ref.1, bf16[128,896]{1,0:T(8,128)(2,1)} %wu_ref.1), custom_call_target="tpu_custom_call" | custom-call | tf_op jit(solution)/shard_map/step/pallas_call | solution.py:518
  78.3 0.8 %slice_bitcast_fusion = (bf16[128,896]{1,0:T(8,128)(2,1)}, bf16[128,896]{1,0:T(8,128)(2,1)}) fusion(bf16[2,128,896]{2,1,0:T(8,128)(2,1)S(1)} %get-tuple-element.6), kind=kLoop, calls=%fused_computation | loop fusion | bytes 917504 | tf_op jit(solution)/shard_map/squeeze | solution.py:532
  79.1 0.6 copy.8

commit v6 on v5

--- a/solution.py
+++ b/solution.py
@@ -35,7 +35,7 @@
     w_s, w_r, p_s, p_r, ys_s, ys_r, g_s, g_r, k_s, k_r, d_s, d_r, zs_s, zs_r, e_s, e_r = take(16)
 
     tok, dmod, z = lax.axis_index("tok"), lax.axis_index("dmod"), lax.axis_index("hid")
-    xl, y, xh, c = tok // ny, tok % ny, dmod // 2, dmod % 2
+    xl, y, xh, c = lax.div(tok, ny), lax.rem(tok, ny), lax.div(dmod, 2), lax.rem(dmod, 2)
     other = 1 - c
     x = dmod - c + xl
     q = 2 * xl + xh
@@ -48,13 +48,14 @@
         return {"tok": xl_ * ny + y_, "dmod": xh_ * 2 + c_, "hid": z_}
 
     def along_x(k):
-        xk = (x + 4 + k) % 4
-        return 2 * (xk % 2) + xk // 2, at(xl_=xk % 2, xh_=xk // 2)
+        xk = lax.rem(x + 4 + k, 4)
+        low, high = lax.rem(xk, 2), lax.div(xk, 2)
+        return 2 * low + high, at(xl_=low, xh_=high)
 
     def along(axis, k):
         if axis == "y":
-            return (y + ny + k) % ny
-        return (z + nz + k) % nz
+            return lax.rem(y + ny + k, ny)
+        return lax.rem(z + nz + k, nz)
 
     def there(axis, k):
         return at(y_=along("y", k)) if axis == "y" else at(z_=along("z", k))
@@ -130,7 +131,7 @@
             pending.append(send(own, own, w_s.at[i, slot], w_r.at[i, slot], along_x(k)[1]))
 
     part = tokens // GROUP
-    turn = z % GROUP
+    turn = lax.rem(z, GROUP)
 
     def part_of(slab, j):
         return slab.at[:, pl.ds(pl.multiple_of(j * part, part), part)]
@@ -162,12 +163,12 @@
         mine = part_of(xg.at[1 - xl], turn)
         arrived(mine, x_r.at[1])
         for k in range(1, GROUP):
-            mate = z - turn + (turn + k) % GROUP
+            mate = z - turn + lax.rem(turn + k, GROUP)
             pending.append(send(mine, mine, t_s.at[k - 1], t_r.at[k - 1], at(z_=mate)))
 
     def features_done():
         for k in range(1, GROUP):
-            arrived(part_of(xg.at[1 - xl], (turn + GROUP - k) % GROUP), t_r.at[k - 1])
+            arrived(part_of(xg.at[1 - xl], lax.rem(turn + GROUP - k, GROUP)), t_r.at[k - 1])
 
         @pl.when(jnp.logical_not(home))
         def _():
@@ -200,7 +201,7 @@
 
     def reduce_start(axis, hops, src, far, near, anti, s_sem, r_sem, cuts=1):
         place = lambda k: along(axis, k)
-        way = 2 * (along(axis, 0) % 2) - 1
+        way = 2 * lax.rem(y if axis == "y" else z, 2) - 1
         lines = src.shape[1] // cuts
         for cut in range(cuts):
             part = pl.ds(cut * lines, lines)
@@ -225,7 +226,7 @@
                 )
 
     def reduce_relay(axis, hops, own, far, anti, hubs, r_sem, deliver, cut=0, cuts=1):
-        odd = along(axis, 0) % 2
+        odd = lax.rem(y if axis == "y" else z, 2)
         lines = hubs.shape[1] // cuts
         part = pl.ds(cut * lines, lines)
         for j in range(1, hops):
@@ -245,7 +246,7 @@
             deliver(si, along(axis, way * hops))
 
     def reduce_near(axis, hops, own, near, r_sem, cuts=1):
-        total = own(along(axis, 0), slice(None))
+        total = own(y if axis == "y" else z, slice(None))
         for j in range(1, hops):
             for si in range(2):
                 slot = (2 * hops - 1) * cuts + si * (hops - 1) + j - 1
@@ -306,7 +307,7 @@
             for j in range(1, y_hops):
                 slot = s * (j + y_hops) % ny - 1
                 pending.append(send(block, block, g_s.at[i, slot], g_r.at[i, slot], there("y", s * j)))
-        way = 2 * (y % 2) - 1
+        way = 2 * lax.rem(y, 2) - 1
         block = gb[i].at[c, along("y", -way * y_hops)]
         slot = 2 * y_hops - 1
         pending.append(

time: 79.9 us -> 79.9 us (level)
  no operation moved by 1% of the time
where the time goes in v6:
time: 79.9 us; the launch traced here: 79.7 us
  Pallas kernels  77.6 us (97%)
  local copies, waits for them, and re-layouts  1.41 us (2%)
    pallas_call x1, Pallas kernels, shards(): pl.pallas_call(functools.partial(kernel, ny, nz, cols), out_shape=(jax.Sh...  77.6 us

profile of v6, /device:TPU:1, one launch (start us, length us, event | category | flops | bytes accessed | tf_op | source)
XLA Modules:
  0.0 79.7 jit_solution(2586519994319448002)
XLA Ops:
  0.6 77.6 %step.1 = (bf16[24,512]{1,0:T(8,128)(2,1)S(1)}, bf16[2,128,896]{2,1,0:T(8,128)(2,1)S(1)}) custom-call(bf16[384,512]{1,0:T(8,128)(2,1)} %x_ref.1, bf16[384,896]{1,0:T(8,128)(2,1)} %gh_ref.1, bf16[128,896]{1,0:T(8,128)(2,1)} %wg_ref.1, bf16[128,896]{1,0:T(8,128)(2,1)} %wu_ref.1), custom_call_target="tpu_custom_call" | custom-call | tf_op jit(solution)/shard_map/step/pallas_call | solution.py:519
  78.3 0.8 %slice_bitcast_fusion = (bf16[128,896]{1,0:T(8,128)(2,1)}, bf16[128,896]{1,0:T(8,128)(2,1)}) fusion(bf16[2,128,896]{2,1,0:T(8,128)(2,1)S(1)} %get-tuple-element.6), kind=kLoop, calls=%fused_computation | loop fusion | bytes 917504 | tf_op jit(solution)/shard_map/squeeze | solution.py:533
  79.1 0.6 copy.8
